TPU v7x, 32 devices: a whole 2x2x4 slice. The times are simulated.
32 devices in a mesh: group: 4 (over z), dev: 8 (over y, x, core).
Axes of the slice: x: 2, y: 2, z: 4, core: 2. Of those that a mesh axis runs over, the one named last changes fastest.
Arguments:
- tokens: bfloat16 [4096, 3584], P(('group', 'dev')), may hold values from -1.5 to 1.5
- out_grad: bfloat16 [4096, 3584], P(('group', 'dev')), may hold values from -0.59765625 to 0.59765625
- gate_weights: bfloat16 [4096, 8], P(('group', 'dev')), may hold values from 0.099609375 to 1
- expert_ids: int32 [4096, 8], P(('group', 'dev')), may hold values from 0 to 31, as said below
- slot_ids: int32 [4096, 8], P(('group', 'dev')), may hold values from 0 to 39, as said below
- up_weight: bfloat16 [32, 3584, 1024], P(('group', 'dev')), may hold values from -0.40039062 to 0.40039062
- down_weight: bfloat16 [32, 1024, 3584], P(('group', 'dev')), may hold values from -0.1875 to 0.1875
Outputs:
- token_grad: bfloat16 [4096, 3584], P(('group', 'dev'))
- gate_grad: bfloat16 [4096, 8], P(('group', 'dev'))
Inputs may be any that keep to these rules, and one draw needn't show every extreme that they name: `expert_ids`: expert e lies in group e // 8 and on the device of index e along group+dev. Each token names 8 different experts, 4 in each of exactly 2 groups. In the rows of one device no expert is named more than 40 times and some expert exactly 40 times; no group is named by more than 80 rows and some group by exactly 80. `slot_ids`: in the rows of one device, two entries that name the same expert have different slots.
All inputs are finite; a program needn't handle non-finite values.
Results may differ from a plain program's by a relative error of at most 0.009.
Values may be sent and summed in bfloat16 or wider, within the bound.
A program may use at most 192 MiB of HBM per device.

v0:
```python
import jax
import jax.numpy as jnp
from jax import lax
from jax.sharding import PartitionSpec as P

TOPK = 8


def silu_slope(values):
    sigmoid_up = jax.nn.sigmoid(values)
    return sigmoid_up * (1.0 + values * (1.0 - sigmoid_up))


def expert_rows(token_rows, grad_rows, gate_rows, up_matrix, down_matrix):
    raised = jnp.dot(token_rows, up_matrix, preferred_element_type=jnp.float32)
    backward = lax.dot_general(
        grad_rows, down_matrix, (((1,), (1,)), ((), ())), preferred_element_type=jnp.float32
    )
    gate_grad = jnp.sum(jax.nn.silu(raised) * backward, axis=1).astype(jnp.bfloat16)
    inner_grad = (gate_rows.astype(jnp.float32)[:, None] * backward * silu_slope(raised)).astype(
        jnp.bfloat16
    )
    contrib = lax.dot_general(
        inner_grad, up_matrix, (((1,), (1,)), ((), ())), preferred_element_type=jnp.float32
    ).astype(jnp.bfloat16)
    return (contrib, gate_grad)


def shards(tokens, out_grad, gate_weights, expert_ids, slot_ids, up_weight, down_weight):
    rows_dev = tokens.shape[0]
    features = tokens.shape[1]
    groups = lax.axis_size("group")
    per_group = lax.axis_size("dev")
    experts = groups * per_group
    capacity = 5 * rows_dev * TOPK // (4 * experts)
    slots_all = experts * capacity
    entries = rows_dev * TOPK
    up_matrix = up_weight[0]
    down_matrix = down_weight[0]
    group_of = expert_ids // per_group
    zero_row = jnp.zeros((1, features), jnp.bfloat16)
    token_pad = jnp.concatenate([tokens, zero_row])
    grad_pad = jnp.concatenate([out_grad, zero_row])
    gate_flat = jnp.concatenate([gate_weights.reshape(-1), jnp.zeros((1,), jnp.bfloat16)])
    target = (expert_ids * capacity + slot_ids).reshape(-1)
    slot_table = (
        jnp.full((slots_all,), entries, jnp.int32)
        .at[target]
        .set(jnp.arange(entries, dtype=jnp.int32))
    )
    anchor = slot_table // TOPK
    arrived = (
        lax.all_to_all(
            token_pad[anchor].reshape(experts, capacity, features),
            ("group", "dev"),
            split_axis=0,
            concat_axis=0,
            tiled=True,
        ),
        lax.all_to_all(
            grad_pad[anchor].reshape(experts, capacity, features),
            ("group", "dev"),
            split_axis=0,
            concat_axis=0,
            tiled=True,
        ),
        lax.all_to_all(
            gate_flat[slot_table].reshape(experts, capacity),
            ("group", "dev"),
            split_axis=0,
            concat_axis=0,
            tiled=True,
        ),
    )
    contrib, gate_rows = expert_rows(
        arrived[0].reshape(slots_all, features),
        arrived[1].reshape(slots_all, features),
        arrived[2].reshape(slots_all),
        up_matrix,
        down_matrix,
    )
    returned_rows = (
        lax.all_to_all(
            contrib.reshape(experts, capacity, features),
            ("group", "dev"),
            split_axis=0,
            concat_axis=0,
            tiled=True,
        ),
        lax.all_to_all(
            gate_rows.reshape(experts, capacity),
            ("group", "dev"),
            split_axis=0,
            concat_axis=0,
            tiled=True,
        ),
    )
    gathered = (
        returned_rows[0].reshape(slots_all, features)[target].reshape(rows_dev, TOPK, features)
    )
    gate_grad = returned_rows[1].reshape(-1)[target].reshape(rows_dev, TOPK)
    same_group = group_of == group_of[:, :1]
    selector = jnp.stack([same_group, jnp.logical_not(same_group)], axis=1).astype(jnp.bfloat16)
    halves = jnp.einsum(
        "tpk,tkd->tpd", selector, gathered, preferred_element_type=jnp.float32
    ).astype(jnp.bfloat16)
    token_grad = jnp.sum(halves.astype(jnp.float32), axis=1).astype(jnp.bfloat16)
    return (token_grad, gate_grad)


def solution(mesh):
    in_specs = (
        P(("group", "dev"), None),
        P(("group", "dev"), None),
        P(("group", "dev"), None),
        P(("group", "dev"), None),
        P(("group", "dev"), None),
        P(("group", "dev"), None, None),
        P(("group", "dev"), None, None),
    )
    out_specs = (P(("group", "dev"), None), P(("group", "dev"), None))
    return jax.shard_map(shards, mesh=mesh, in_specs=in_specs, out_specs=out_specs, check_vma=False)
```

profile of v0, /device:TPU:0, one launch (start us, length us, event | category | flops | bytes accessed | tf_op | source)
XLA Modules:
  0.0 726.4 jit_solution(14123534415179853554)
XLA Ops:
  0.6 0.7 multiply_add_fusion
  1.3 0.1 copy.29
  1.4 0.1 reshape.95
  1.6 4.3 scatter_custom_fusion
  5.9 0.8 copy.28
  6.7 0.1 reshape.94
  6.8 8.0 %gather_fusion = bf16[1280]{0:T(1024)(128)(2,1)S(1)} fusion(bf16[1025]{0:T(1024)(128)(2,1)S(1)} %pad_maximum_fusion, s32[2048]{0:T(1024)S(1)} %get-tuple-element.17), kind=kCustom, calls=%fused_computation | custom fusion | bytes 10240 | tf_op jit(solution)/shard_map/gather | solution.py:68
  14.8 0.7 all_to_all.25
  15.5 7.3 %all-to-all-start = ((bf16[32,1,40]{2,1,0:T(2,128)(2,1)}), bf16[32,1,40]{2,1,0:T(2,128)(2,1)S(1)}, u32[]{:S(2)}, u32[]{:S(2)}) async-start(bf16[32,1,40]{2,1,0:T(2,128)(2,1)} %all_to_all.25), calls=%async_computation | async-start | bytes 32768 | tf_op jit(solution)/shard_map/all_to_all | solution.py:67
  22.8 1.2 concatenate.11
  24.1 7.9 %gather_fusion.2 = bf16[1280,3584]{1,0:T(8,128)(2,1)} fusion(bf16[129,3584]{1,0:T(8,128)(2,1)S(1)} %concatenate.11, s32[2048]{0:T(1024)S(1)} %get-tuple-element.16), kind=kCustom, calls=%fused_computation.2 | custom fusion | bytes 18355200 | tf_op jit(solution)/shard_map/gather | solution.py:54
  32.0 0.0 all-to-all-done
  32.0 0.0 copy-start
  32.0 6.0 all-to-all-start.2
  38.0 0.0 copy-done
  38.0 0.1 concatenate.10
  38.0 7.9 %gather_fusion.1 = bf16[1280,3584]{1,0:T(8,128)(2,1)} fusion(bf16[129,3584]{1,0:T(8,128)(2,1)S(1)} %concatenate.10, s32[2048]{0:T(1024)S(1)} %get-tuple-element.16), kind=kCustom, calls=%fused_computation.1 | custom fusion | bytes 18355200 | tf_op jit(solution)/shard_map/gather | solution.py:61
  45.9 195.4 %all-to-all-done.2 = bf16[32,40,3584]{2,1,0:T(8,128)(2,1)} async-done(((bf16[32,40,3584]{2,1,0:T(8,128)(2,1)}), bf16[32,40,3584]{2,1,0:T(8,128)(2,1)}, u32[]{:S(2)}, u32[]{:S(2)}) %all-to-all-start.2) | async-done | bytes 9175072 | tf_op jit(solution)/shard_map/all_to_all | solution.py:53
  241.3 3.9 all-to-all-start.1
  245.2 0.1 convert_reduce_fusion
  245.3 0.1 reshape.105
  245.4 15.8 %fusion.3 = f32[1280,1024]{0,1:T(8,128)} fusion(bf16[1280,3584]{1,0:T(8,128)(2,1)} %bitcast.8, bf16[1,3584,1024]{2,1,0:T(8,128)(2,1)} %param.12), kind=kOutput, calls=%fused_computation.10 | convolution fusion | flops 9395240960 | bytes 21757952 | tf_op jit(solution)/shard_map/dot_general | solution.py:15
  261.1 187.6 %all-to-all-done.1 = bf16[32,40,3584]{2,1,0:T(8,128)(2,1)} async-done(((bf16[32,40,3584]{2,1,0:T(8,128)(2,1)}), bf16[32,40,3584]{2,1,0:T(8,128)(2,1)}, u32[]{:S(2)}, u32[]{:S(2)}) %all-to-all-start.1) | async-done | bytes 9175072 | tf_op jit(solution)/shard_map/all_to_all | solution.py:60
  448.7 17.2 %multiply_reduce_fusion = (bf16[1280]{0:T(1024)(128)(2,1)S(1)}, f32[1280,1024]{0,1:T(8,128)}) fusion(f32[1280,1024]{0,1:T(8,128)} %fusion.3, bf16[1280,3584]{1,0:T(8,128)(2,1)} %bitcast.5, bf16[1,1024,3584]{2,1,0:T(8,128)(2,1)} %param.13), kind=kOutput, calls=%fused_computation.14 | convolution fusion | flops 9403104256 | bytes 27003392 | tf_op jit(solution)/shard_map/dot_general | solution.py:16
  465.9 0.7 convert_element_type.44
  466.6 2.8 all-to-all-start.4
  469.4 20.5 %convolution_convert_fusion = bf16[1280,3584]{1,0:T(8,128)(2,1)} fusion(bf16[1,3584,1024]{2,1,0:T(8,128)(2,1)} %param.12, f32[1280,1024]{0,1:T(8,128)} %fusion.3, f32[1280,1024]{0,1:T(8,128)} %get-tuple-element.15, f32[1280]{0:T(1024)S(1)} %reshape.105), kind=kOutput, calls=%fused_computation.6 | convolution fusion | flops 9412935680 | bytes 27005952 | tf_op jit(solution)/shard_map/dot_general | solution.py:23
  489.9 0.0 all-to-all-done.4
  489.9 6.0 all-to-all-start.3
  495.9 0.2 copy.31
  496.1 0.1 reduce.2
  496.2 0.1 reshape.103
  496.3 6.8 gather_fusion.4
  503.1 0.1 reshape.104
  503.2 0.7 copy.33
  503.8 195.3 %all-to-all-done.3 = bf16[32,40,3584]{2,1,0:T(8,128)(2,1)} async-done(((bf16[32,40,3584]{2,1,0:T(8,128)(2,1)}), bf16[32,40,3584]{2,1,0:T(8,128)(2,1)}, u32[]{:S(2)}, u32[]{:S(2)}) %all-to-all-start.3) | async-done | bytes 9175072 | tf_op jit(solution)/shard_map/all_to_all | solution.py:83
  699.2 18.6 %gather_fusion.3 = bf16[1024,3584]{1,0:T(8,128)(2,1)} fusion(bf16[1280,3584]{1,0:T(8,128)(2,1)} %bitcast.11, s32[1024]{0:T(1024)S(1)} %broadcast_clamp_fusion), kind=kCustom, calls=%fused_computation.3 | custom fusion | bytes 14684160 | tf_op jit(solution)/shard_map/gather | solution.py:99
  717.8 8.7 %fusion.12 = bf16[128,3584]{1,0:T(8,128)(2,1)} fusion(pred[128,2,8]{2,1,0:T(4,128)(4,1)S(1)} %copy.31, bf16[1024,3584]{1,0:T(8,128)(2,1)} %gather_fusion.3), kind=kOutput, calls=%fused_computation.20 | convolution fusion | flops 16056320 | bytes 8259584 | tf_op jit(solution)/shard_map/tpk,tkd->tpd/dot_general | solution.py:104
  (9 shorter events, 0.1 us)
Async XLA Ops:
  15.5 16.5 %all-to-all-start = ((bf16[32,1,40]{2,1,0:T(2,128)(2,1)}), bf16[32,1,40]{2,1,0:T(2,128)(2,1)S(1)}, u32[]{:S(2)}, u32[]{:S(2)}) async-start(bf16[32,1,40]{2,1,0:T(2,128)(2,1)} %all_to_all.25), calls=%async_computation | async-start | bytes 32768 | tf_op jit(solution)/shard_map/all_to_all | solution.py:67
  32.0 6.0 copy-start
  32.0 209.3 %all-to-all-start.2 = ((bf16[32,40,3584]{2,1,0:T(8,128)(2,1)}), bf16[32,40,3584]{2,1,0:T(8,128)(2,1)}, u32[]{:S(2)}, u32[]{:S(2)}) async-start(bf16[32,40,3584]{2,1,0:T(8,128)(2,1)} %bitcast.33), calls=%async_computation.2 | async-start | bytes 18350080 | tf_op jit(solution)/shard_map/all_to_all | solution.py:53
  241.3 207.4 %all-to-all-start.1 = ((bf16[32,40,3584]{2,1,0:T(8,128)(2,1)}), bf16[32,40,3584]{2,1,0:T(8,128)(2,1)}, u32[]{:S(2)}, u32[]{:S(2)}) async-start(bf16[32,40,3584]{2,1,0:T(8,128)(2,1)} %bitcast.32), calls=%async_computation.1 | async-start | bytes 18350080 | tf_op jit(solution)/shard_map/all_to_all | solution.py:60
  466.6 23.3 %all-to-all-start.4 = ((bf16[32,1,40]{2,1,0:T(2,128)(2,1)}), bf16[32,1,40]{2,1,0:T(2,128)(2,1)S(1)}, u32[]{:S(2)}, u32[]{:S(2)}) async-start(bf16[32,1,40]{2,1,0:T(2,128)(2,1)} %convert_element_type.44), calls=%async_computation.4 | async-start | bytes 32768 | tf_op jit(solution)/shard_map/all_to_all | solution.py:90
  489.9 209.3 %all-to-all-start.3 = ((bf16[32,40,3584]{2,1,0:T(8,128)(2,1)}), bf16[32,40,3584]{2,1,0:T(8,128)(2,1)}, u32[]{:S(2)}, u32[]{:S(2)}) async-start(bf16[32,40,3584]{2,1,0:T(8,128)(2,1)} %bitcast.34), calls=%async_computation.3 | async-start | bytes 18350080 | tf_op jit(solution)/shard_map/all_to_all | solution.py:83
where the time goes:
time: 727 us; the launch traced here: 726 us
  waiting for transfers between devices  578 us (80%)
  matrix products  62.1 us (9%)
  local copies, waits for them, and re-layouts  58.4 us (8%)
  starting transfers between devices  25.9 us (4%)
    all_to_all x1, waiting for transfers between devices, shards(): lax.all_to_all(token_pad[anchor].reshape(experts, capacity, features), ('...  195 us
    all_to_all x1, waiting for transfers between devices, shards(): lax.all_to_all(contrib.reshape(experts, capacity, features), ('group', 'd...  195 us
    all_to_all x1, waiting for transfers between devices, shards(): lax.all_to_all(grad_pad[anchor].reshape(experts, capacity, features), ('g...  188 us
    dot_general x1, matrix products, expert_rows(): lax.dot_general(inner_grad, up_matrix, (((1,), (1,)), ((), ())), preferre...  20.5 us
    gather x1, local copies, waits for them, and re-layouts, shards(): returned_rows[0].reshape(slots_all, features)[target]  18.6 us
    dot_general x1, matrix products, expert_rows(): lax.dot_general(grad_rows, down_matrix, (((1,), (1,)), ((), ())), preferr...  17.2 us
    dot_general x1, matrix products, expert_rows(): raised = jnp.dot(token_rows, up_matrix, preferred_element_type=jnp.float32)  15.8 us
  transfers between devices with their start and end apart: 5, of which 3 were waited for; matrix products, arithmetic and copies ran while one was open for 8% of the time, Pallas kernels for 0%

commit v1 on v0

--- a/solution.py
+++ b/solution.py
@@ -1,9 +1,17 @@
+import functools
+
 import jax
 import jax.numpy as jnp
 from jax import lax
+from jax.experimental import pallas as pl
+from jax.experimental.pallas import tpu as pltpu
 from jax.sharding import PartitionSpec as P
 
 TOPK = 8
+MESH = pl.DeviceIdType.MESH
+GROUPS = 4
+PEERS = 8
+MIB = 1024 * 1024
 
 
 def silu_slope(values):
@@ -24,6 +32,366 @@
         inner_grad, up_matrix, (((1,), (1,)), ((), ())), preferred_element_type=jnp.float32
     ).astype(jnp.bfloat16)
     return (contrib, gate_grad)
+
+
+class Place:
+    def __init__(self):
+        self.group = lax.axis_index("group")
+        self.dev = lax.axis_index("dev")
+        core = self.dev % 2
+        side = (self.dev // 2) % 2
+        row = self.dev // 4
+        self.sib = self.dev + 1 - 2 * core
+        self.xn = self.dev + 2 - 4 * side
+        self.yn = self.dev + 4 - 8 * row
+        self.diag = self.xn + 4 - 8 * row
+        self.off_sib = 1 - 2 * core
+
+    def source(self, k):
+        return lax.rem(self.group + k, GROUPS)
+
+    def barrier(self):
+        sem = pltpu.get_barrier_semaphore()
+        for peer in (self.sib, self.xn, self.yn):
+            pl.semaphore_signal(sem, inc=1, device_id=(self.group, peer), device_id_type=MESH)
+        for k in range(1, GROUPS):
+            pl.semaphore_signal(
+                sem, inc=1, device_id=(self.source(k), self.dev), device_id_type=MESH
+            )
+        pl.semaphore_wait(sem, GROUPS + 2)
+
+
+def dispatch_kernel(tok, grad, ytok, ygrad, local_sem, zs, zr, ss, rs):
+    at = Place()
+    at.barrier()
+    pairs = ((tok, ytok), (grad, ygrad))
+    g, d = at.group, at.dev
+
+    def local(a):
+        src, dst = pairs[a]
+        return pltpu.make_async_copy(src.at[g], dst.at[g, d], local_sem.at[a])
+
+    def zcopy(a, k):
+        src, dst = pairs[a]
+        target = lax.rem(g + GROUPS - k, GROUPS)
+        return pltpu.make_async_remote_copy(
+            src_ref=src.at[target], dst_ref=dst.at[g, d],
+            send_sem=zs.at[a, k], recv_sem=zr.at[a, k],
+            device_id=(target, d), device_id_type=MESH,
+        )
+
+    def copy(a, k, origin, slot, rel, peer):
+        buf = pairs[a][1].at[at.source(k), origin]
+        return pltpu.make_async_remote_copy(
+            src_ref=buf, dst_ref=buf,
+            send_sem=ss.at[a, k, slot], recv_sem=rs.at[a, k, rel],
+            device_id=(g, peer), device_id_type=MESH,
+        )
+
+    def sends(a, k):
+        first = [
+            copy(a, k, d, 0, 2, at.xn),
+            copy(a, k, d, 1, 4, at.yn),
+            copy(a, k, d, 2, 1, at.sib),
+        ]
+        from_x = [copy(a, k, at.xn, 3, 3, at.sib)]
+        from_y = [copy(a, k, at.yn, 4, 5, at.sib)]
+        if k % 2 == 0:
+            from_x.insert(0, copy(a, k, at.xn, 5, 6, at.yn))
+        else:
+            from_y.insert(0, copy(a, k, at.yn, 5, 6, at.xn))
+        last = [copy(a, k, at.diag, 6, 7, at.sib)]
+        return first, from_x, from_y, last
+
+    def own(a, k):
+        if k == 0:
+            local(a).wait()
+        else:
+            zcopy(a, k).wait_recv()
+        for c in sends(a, k)[0]:
+            c.start()
+
+    def forward(a, k):
+        parts = sends(a, k)
+        copy(a, k, at.xn, 0, 2, at.xn).wait_recv()
+        for c in parts[1]:
+            c.start()
+        copy(a, k, at.yn, 1, 4, at.yn).wait_recv()
+        for c in parts[2]:
+            c.start()
+
+    def forward_last(a, k):
+        copy(a, k, at.diag, 5, 6, at.xn).wait_recv()
+        for c in sends(a, k)[3]:
+            c.start()
+
+    order = [(0, 0), (1, 0), (0, 1), (0, 2), (0, 3), (1, 1), (1, 2), (1, 3)]
+    for a in range(2):
+        local(a).start()
+    for k in range(1, GROUPS):
+        zcopy(0, k).start()
+    for i in range(len(order) + 2):
+        if i < len(order):
+            own(*order[i])
+        if i == 1:
+            for k in range(1, GROUPS):
+                zcopy(1, k).start()
+        if 1 <= i <= len(order):
+            forward(*order[i - 1])
+        if i >= 2:
+            forward_last(*order[i - 2])
+    for a, k in order:
+        copy(a, k, at.sib, 2, 1, at.sib).wait_recv()
+        copy(a, k, at.xn + at.off_sib, 3, 3, at.sib).wait_recv()
+        copy(a, k, at.yn + at.off_sib, 4, 5, at.sib).wait_recv()
+        copy(a, k, at.diag + at.off_sib, 6, 7, at.sib).wait_recv()
+        for part in sends(a, k):
+            for c in part:
+                c.wait_send()
+        if k:
+            zcopy(a, k).wait_send()
+
+
+def dispatch(tok, grad):
+    groups, rows, features = tok.shape
+    out = jax.ShapeDtypeStruct((groups, PEERS, rows, features), jnp.bfloat16)
+    anywhere = pl.BlockSpec(memory_space=pl.ANY)
+    return pl.pallas_call(
+        dispatch_kernel,
+        out_shape=(out, out),
+        in_specs=[anywhere, anywhere],
+        out_specs=(anywhere, anywhere),
+        scratch_shapes=[
+            pltpu.SemaphoreType.DMA((2,)),
+            pltpu.SemaphoreType.DMA((2, GROUPS)),
+            pltpu.SemaphoreType.DMA((2, GROUPS)),
+            pltpu.SemaphoreType.DMA((2, GROUPS, 7)),
+            pltpu.SemaphoreType.DMA((2, GROUPS, 8)),
+        ],
+        compiler_params=pltpu.CompilerParams(
+            collective_id=0, has_side_effects=True, vmem_limit_bytes=4 * MIB
+        ),
+    )(tok, grad)
+
+
+def combine_kernel(
+    rows, inner, up, out, part, sib, dbuf, xbuf, ybuf, local_sem, zs, zr, ss, rs, ps, pr
+):
+    at = Place()
+    g, d = at.group, at.dev
+    features = up.shape[0]
+    tile = 512
+    at.barrier()
+
+    def product(k):
+        lines = inner[at.source(k)]
+
+        @pl.loop(0, features // tile)
+        def _(n):
+            cols = pl.ds(pl.multiple_of(n * tile, tile), tile)
+            block = lax.dot_general(
+                lines, up[cols, :], (((1,), (1,)), ((), ())),
+                preferred_element_type=jnp.float32,
+            ).astype(jnp.bfloat16)
+            part[k, :, :, cols] = block.reshape(PEERS, rows, tile)
+
+    chips = (at.dev, at.xn, at.yn, at.diag)
+
+    def pair(k, i):
+        return pltpu.make_async_remote_copy(
+            src_ref=part.at[k, chips[i] + at.off_sib], dst_ref=sib.at[k, i],
+            send_sem=ps.at[k, i], recv_sem=pr.at[k, i],
+            device_id=(g, at.sib), device_id_type=MESH,
+        )
+
+    def to(k, slot, origin, buf, peer):
+        return pltpu.make_async_remote_copy(
+            src_ref=part.at[k, origin], dst_ref=buf.at[k],
+            send_sem=ss.at[k, slot], recv_sem=rs.at[k, slot],
+            device_id=(g, peer), device_id_type=MESH,
+        )
+
+    def to_x(k):
+        return to(k, 0, at.xn, xbuf, at.xn)
+
+    def to_y(k):
+        return to(k, 1, at.yn, ybuf, at.yn)
+
+    def to_far(k):
+        return to(k, 2, at.diag, dbuf, at.xn if k % 2 == 0 else at.yn)
+
+    def add(k, origin, *terms):
+        @pl.loop(0, rows // 16)
+        def _(r):
+            lines = pl.ds(pl.multiple_of(r * 16, 16), 16)
+            total = part[k, origin, lines, :].astype(jnp.float32)
+            for buf, index in terms:
+                total = total + buf[index + (lines,)].astype(jnp.float32)
+            part[k, origin, lines, :] = total.astype(jnp.bfloat16)
+
+    def start_pairs(k):
+        for i in (3, 1, 2, 0):
+            pair(k, i).start()
+
+    def first(k):
+        for i in (3, 1, 2, 0):
+            pair(k, i).wait_recv()
+            if i == 3:
+                add(k, at.diag, (sib, (k, 3)))
+                to_far(k).start()
+            elif i == 1:
+                add(k, at.xn, (sib, (k, 1)))
+                if k % 2 == 0:
+                    to_x(k).start()
+            elif i == 2:
+                add(k, at.yn, (sib, (k, 2)))
+                if k % 2 == 1:
+                    to_y(k).start()
+
+    def second(k):
+        to_far(k).wait_recv()
+        if k % 2 == 0:
+            add(k, at.yn, (dbuf, (k,)))
+            to_y(k).start()
+        else:
+            add(k, at.xn, (dbuf, (k,)))
+            to_x(k).start()
+
+    def home(k):
+        target = at.source(k)
+        return pltpu.make_async_remote_copy(
+            src_ref=part.at[k, d], dst_ref=out.at[g],
+            send_sem=zs.at[k], recv_sem=zr.at[k],
+            device_id=(target, d), device_id_type=MESH,
+        )
+
+    def local():
+        return pltpu.make_async_copy(part.at[0, d], out.at[g], local_sem)
+
+    def third(k):
+        to_x(k).wait_recv()
+        to_y(k).wait_recv()
+        add(k, d, (sib, (k, 0)), (xbuf, (k,)), (ybuf, (k,)))
+        if k:
+            home(k).start()
+        else:
+            local().start()
+
+    order = (2, 1, 3, 0)
+    for i in range(len(order) + 3):
+        if i < len(order):
+            product(order[i])
+            start_pairs(order[i])
+        if 1 <= i <= len(order):
+            first(order[i - 1])
+        if 2 <= i <= len(order) + 1:
+            second(order[i - 2])
+        if i >= 3:
+            third(order[i - 3])
+    for k in order:
+        for i in range(4):
+            pair(k, i).wait_send()
+        to_x(k).wait_send()
+        to_y(k).wait_send()
+        to_far(k).wait_send()
+        if k:
+            home(k).wait_send()
+            home(k).wait_recv()
+    local().wait()
+
+
+def combine(inner, up_matrix, rows):
+    features = up_matrix.shape[0]
+    whole = pl.BlockSpec(memory_space=pltpu.VMEM)
+    hop = pltpu.VMEM((GROUPS, rows, features), jnp.bfloat16)
+    return pl.pallas_call(
+        functools.partial(combine_kernel, rows),
+        out_shape=jax.ShapeDtypeStruct((GROUPS, rows, features), jnp.bfloat16),
+        in_specs=[whole, whole],
+        out_specs=pl.BlockSpec(memory_space=pl.ANY),
+        scratch_shapes=[
+            pltpu.VMEM((GROUPS, PEERS, rows, features), jnp.bfloat16),
+            pltpu.VMEM((GROUPS, 4, rows, features), jnp.bfloat16),
+            hop,
+            hop,
+            hop,
+            pltpu.SemaphoreType.DMA,
+            pltpu.SemaphoreType.DMA((GROUPS,)),
+            pltpu.SemaphoreType.DMA((GROUPS,)),
+            pltpu.SemaphoreType.DMA((GROUPS, 3)),
+            pltpu.SemaphoreType.DMA((GROUPS, 3)),
+            pltpu.SemaphoreType.DMA((GROUPS, 4)),
+            pltpu.SemaphoreType.DMA((GROUPS, 4)),
+        ],
+        compiler_params=pltpu.CompilerParams(
+            collective_id=1, has_side_effects=True, vmem_limit_bytes=58 * MIB
+        ),
+    )(inner, up_matrix)
+
+
+def grouped(tokens, out_grad, gate_weights, expert_ids, slot_ids, up_weight, down_weight):
+    rows_dev, features = tokens.shape
+    hidden = up_weight.shape[2]
+    experts = GROUPS * PEERS
+    rows = 5 * rows_dev // 8
+    up_matrix = up_weight[0]
+    down_matrix = down_weight[0]
+    names = expert_ids[:, :, None] == jnp.arange(experts, dtype=jnp.int32)
+    in_group = jnp.any(
+        (expert_ids // PEERS)[:, :, None] == jnp.arange(GROUPS, dtype=jnp.int32), axis=1
+    )
+    before = jnp.arange(rows_dev)[:, None] > jnp.arange(rows_dev)[None, :]
+    rank = jnp.dot(
+        before.astype(jnp.bfloat16), in_group.astype(jnp.bfloat16),
+        preferred_element_type=jnp.float32,
+    ).astype(jnp.int32)
+    pick = jnp.logical_and(
+        in_group[:, :, None],
+        rank[:, :, None] == jnp.arange(rows, dtype=jnp.int32),
+    ).astype(jnp.bfloat16)
+
+    def packed(values):
+        return jnp.einsum(
+            "tgp,td->gpd", pick, values, preferred_element_type=jnp.float32
+        ).astype(jnp.bfloat16)
+
+    gate_table = jnp.sum(
+        jnp.where(names, gate_weights.astype(jnp.float32)[:, :, None], 0.0), axis=1
+    ).astype(jnp.bfloat16)
+    gate_send = jnp.einsum(
+        "tgp,tge->gep", pick, gate_table.reshape(rows_dev, GROUPS, PEERS),
+        preferred_element_type=jnp.float32,
+    ).astype(jnp.bfloat16)
+    gate_rows = lax.all_to_all(
+        gate_send.reshape(experts, rows), ("group", "dev"), 0, 0, tiled=True
+    ).reshape(-1)
+    token_rows, grad_rows = dispatch(packed(tokens), packed(out_grad))
+    raised = jnp.dot(
+        token_rows.reshape(-1, features), up_matrix, preferred_element_type=jnp.float32
+    )
+    backward = lax.dot_general(
+        grad_rows.reshape(-1, features), down_matrix, (((1,), (1,)), ((), ())),
+        preferred_element_type=jnp.float32,
+    )
+    gate_out = jnp.sum(jax.nn.silu(raised) * backward, axis=1).astype(jnp.bfloat16)
+    inner = (gate_rows.astype(jnp.float32)[:, None] * backward * silu_slope(raised)).astype(
+        jnp.bfloat16
+    )
+    gate_back = lax.all_to_all(
+        gate_out.reshape(experts, rows), ("group", "dev"), 0, 0, tiled=True
+    )
+    halves = combine(inner.reshape(GROUPS, PEERS * rows, hidden), up_matrix, rows)
+    gate_tokens = jnp.einsum(
+        "tgp,gep->tge", pick, gate_back.reshape(GROUPS, PEERS, rows),
+        preferred_element_type=jnp.float32,
+    ).reshape(rows_dev, experts)
+    gate_grad = jnp.sum(jnp.where(names, gate_tokens[:, None, :], 0.0), axis=2).astype(
+        jnp.bfloat16
+    )
+    token_grad = jnp.einsum(
+        "tgp,gpd->td", pick, halves, preferred_element_type=jnp.float32
+    ).astype(jnp.bfloat16)
+    return (token_grad, gate_grad)
 
 
 def shards(tokens, out_grad, gate_weights, expert_ids, slot_ids, up_weight, down_weight):
@@ -119,4 +487,6 @@
         P(("group", "dev"), None, None),
     )
     out_specs = (P(("group", "dev"), None), P(("group", "dev"), None))
-    return jax.shard_map(shards, mesh=mesh, in_specs=in_specs, out_specs=out_specs, check_vma=False)
+    fits = mesh.shape["group"] == GROUPS and mesh.shape["dev"] == PEERS
+    step = grouped if fits else shards
+    return jax.shard_map(step, mesh=mesh, in_specs=in_specs, out_specs=out_specs, check_vma=False)

time: 727 us -> 395 us (0.54)
  waiting for transfers between devices: 578 us -> 7.05 us
  Pallas kernels: 0 us -> 289 us
  local copies, waits for them, and re-layouts: 58.4 us -> 7.32 us
  starting transfers between devices: 25.9 us -> 2.54 us
  other arithmetic: 0.87 us -> 13 us
  blocking collectives: 0 us -> 8.85 us
    all_to_all x5 -> x1, waiting for transfers between devices: 578 us -> 7.05 us  [grouped(): lax.all_to_all(gate_out.reshape(experts, rows), ('group', 'dev'), 0, 0, t...]
    pallas_call x0 -> x2, Pallas kernels: none -> 289 us  [the longest x1 174 us: dispatch(): pl.pallas_call(dispatch_kernel, out_shape=(out, out), in_specs=[anywhere,...]
    gather x5 -> x0, local copies, waits for them, and re-layouts: 49.1 us -> none  [the longest x1 18.6 us: shards(): returned_rows[0].reshape(slots_all, features)[target]]
    all_to_all x5 -> x1, starting transfers between devices: 25.9 us -> 2.54 us  [grouped(): lax.all_to_all(gate_out.reshape(experts, rows), ('group', 'dev'), 0, 0, t...]
    convert_element_type x1 -> x3, other arithmetic: 0.05 us -> 11.6 us  [the longest x1 11.5 us: grouped(): (gate_rows.astype(jnp.float32)[:, None] * backward * silu_slope(raised))....]
    all_to_all x0 -> x1, blocking collectives: none -> 8.85 us  [grouped(): lax.all_to_all(gate_send.reshape(experts, rows), ('group', 'dev'), 0, 0,...]
    dot_general x4 -> x8, matrix products: 62.1 us -> 65.8 us  [the longest x1 32.2 us: grouped(): jnp.dot(token_rows.reshape(-1, features), up_matrix, preferred_element_ty...]
  transfers between devices with their start and end apart: 5 -> 1, of which waited for: 3 -> 1; matrix products, arithmetic and copies ran while one was open for 8% -> 0% of each run, Pallas kernels for 0% -> 0%
where the time goes in v1:
time: 395 us; the launch traced here: 394 us
  Pallas kernels  289 us (73%)
  matrix products  65.8 us (17%)
  other arithmetic  13 us (3%)
  blocking collectives  8.85 us (2%)
  local copies, waits for them, and re-layouts  7.32 us (2%)
  waiting for transfers between devices  7.05 us (2%)
    pallas_call x1, Pallas kernels, dispatch(): pl.pallas_call(dispatch_kernel, out_shape=(out, out), in_specs=[anywhere,...  174 us
    pallas_call x1, Pallas kernels, combine(): pl.pallas_call(functools.partial(combine_kernel, rows), out_shape=jax.Sha...  115 us
    dot_general x1, matrix products, grouped(): jnp.dot(token_rows.reshape(-1, features), up_matrix, preferred_element_ty...  32.2 us
    dot_general x1, matrix products, grouped(): lax.dot_general(grad_rows.reshape(-1, features), down_matrix, (((1,), (1,...  27.2 us
    convert_element_type x1, other arithmetic, grouped(): (gate_rows.astype(jnp.float32)[:, None] * backward * silu_slope(raised))....  11.5 us
    all_to_all x1, blocking collectives, grouped(): lax.all_to_all(gate_send.reshape(experts, rows), ('group', 'dev'), 0, 0,...  8.85 us
  transfers between devices with their start and end apart: 1, of which 1 were waited for; matrix products, arithmetic and copies ran while one was open for 0% of the time, Pallas kernels for 0%

profile of v1, /device:TPU:0, one launch (start us, length us, event | category | flops | bytes accessed | tf_op | source)
XLA Modules:
  0.0 394.4 jit_solution(4106802208467339352)
XLA Ops:
  0.6 0.0 copy-start
  0.6 0.8 add_select_fusion
  1.4 0.1 convolution_convert_fusion.3
  1.6 0.2 copy-done
  1.8 0.7 convolution_convert_fusion.grad
  2.6 1.9 convolution_convert_fusion.1.tok
  4.5 174.4 %shard_map.77 = (bf16[4,8,80,3584]{3,2,1,0:T(8,128)(2,1)S(1)}, bf16[4,8,80,3584]{3,2,1,0:T(8,128)(2,1)S(1)}) custom-call(bf16[4,80,3584]{2,1,0:T(8,128)(2,1)S(1)} %convolution_convert_fusion.1.tok, bf16[4,80,3584]{2,1,0:T(8,128)(2,1)S(1)} %convolution_convert_fusion.grad), custom_call_target="tpu_custom_call" | custom-call | tf_op jit(solution)/shard_map/pallas_call | solution.py:159
  178.9 0.0 copy-start.3
  178.9 6.3 %copy-done.3 = bf16[4,8,80,3584]{3,2,1,0:T(8,128)(2,1)} copy-done((bf16[4,8,80,3584]{3,2,1,0:T(8,128)(2,1)}, bf16[4,8,80,3584]{3,2,1,0:T(8,128)(2,1)S(1)}, u32[]{:S(2)}) %copy-start.3) | copy-done | bytes 18350104
  185.1 0.0 copy-start.2
  185.1 32.2 %fusion.29 = f32[2560,1024]{1,0:T(8,128)} fusion(bf16[2560,3584]{1,0:T(8,128)(2,1)} %bitcast.38, bf16[1,3584,1024]{2,1,0:T(8,128)(2,1)} %param.11), kind=kOutput, calls=%fused_computation.45 | convolution fusion | flops 18790481920 | bytes 36175872 | tf_op jit(solution)/shard_map/dot_general | solution.py:369
  217.4 0.0 copy-done.2
  217.4 0.0 copy-start.5
  217.4 0.0 copy-start.4
  217.4 27.2 %multiply_reduce_fusion = (bf16[2560]{0:T(1024)(128)(2,1)S(1)}, f32[2560,1024]{1,0:T(8,128)}) fusion(f32[2560,1024]{1,0:T(8,128)} %fusion.29, bf16[2560,3584]{1,0:T(8,128)(2,1)} %bitcast.37, bf16[1,1024,3584]{2,1,0:T(8,128)(2,1)} %param.12), kind=kOutput, calls=%fused_computation | convolution fusion | flops 18806208512 | bytes 46666752 | tf_op jit(solution)/shard_map/dot_general | solution.py:372
  244.6 0.7 convert_element_type.73
  245.3 2.5 all-to-all-start.1
  247.9 0.0 copy-done.5
  247.9 7.1 %all-to-all-done.1 = bf16[32,1,80]{2,1,0:T(2,128)(2,1)S(1)} async-done(((bf16[32,1,80]{2,1,0:T(2,128)(2,1)}), bf16[32,1,80]{2,1,0:T(2,128)(2,1)S(1)}, u32[]{:S(2)}, u32[]{:S(2)}) %all-to-all-start.1) | async-done | bytes 5152 | tf_op jit(solution)/shard_map/all_to_all | solution.py:380
  254.9 0.1 convolution_bitcast_fusion.1
  255.1 0.0 copy-done.4
  255.1 0.6 select_reduce_fusion
  255.7 0.2 fusion.3
  255.9 8.8 %all_to_all.15 = bf16[32,1,80]{2,1,0:T(2,128)(2,1)S(1)} all-to-all(bf16[32,1,80]{2,1,0:T(2,128)(2,1)S(1)} %copy.23), channel_id=1, replica_groups=mesh['group'=4,'dev'=8] {'group','dev'}, dimensions={0} | all-to-all | bytes 10240 | tf_op jit(solution)/shard_map/all_to_all | solution.py:365
  264.7 0.1 convert_reduce_fusion
  264.8 0.1 reshape.58
  264.9 0.0 copy-start.1
  264.9 11.5 %multiply_convert_fusion = bf16[2560,1024]{1,0:T(8,128)(2,1)} fusion(f32[2560,1024]{1,0:T(8,128)} %fusion.29, f32[2560,1024]{1,0:T(8,128)} %get-tuple-element.9, f32[2560]{0:T(1024)S(1)} %reshape.58), kind=kLoop, calls=%fused_computation.1 | loop fusion | flops 26214400 | bytes 26224640 | tf_op jit(solution)/shard_map/convert_element_type | solution.py:377
  276.4 114.7 %shard_map.78 = bf16[4,80,3584]{2,1,0:T(8,128)(2,1)} custom-call(bf16[4,640,1024]{2,1,0:T(8,128)(2,1)} %bitcast.39, bf16[3584,1024]{1,0:T(8,128)(2,1)} %bitcast.40), custom_call_target="tpu_custom_call" | custom-call | tf_op jit(solution)/shard_map/pallas_call | solution.py:307
  391.2 3.3 fusion.2
  394.4 0.0 copy-done.1
  (3 shorter events, 0.0 us)
Async XLA Ops:
  0.6 1.2 copy-start
  178.9 6.3 %copy-start.3 = (bf16[4,8,80,3584]{3,2,1,0:T(8,128)(2,1)}, bf16[4,8,80,3584]{3,2,1,0:T(8,128)(2,1)S(1)}, u32[]{:S(2)}) copy-start(bf16[4,8,80,3584]{3,2,1,0:T(8,128)(2,1)S(1)} %get-tuple-element.5) | copy-start | bytes 55050244
  185.1 32.3 %copy-start.2 = (bf16[4,8,80,3584]{3,2,1,0:T(8,128)(2,1)}, bf16[4,8,80,3584]{3,2,1,0:T(8,128)(2,1)S(1)}, u32[]{:S(2)}) copy-start(bf16[4,8,80,3584]{3,2,1,0:T(8,128)(2,1)S(1)} %get-tuple-element.4) | copy-start | bytes 55050244
  217.4 30.5 %copy-start.5 = (bf16[128,8]{0,1:T(8,128)(2,1)S(1)}, bf16[128,8]{0,1:T(8,128)(2,1)}, u32[]{:S(2)}) copy-start(bf16[128,8]{0,1:T(8,128)(2,1)} %param.9) | copy-start | bytes 6148
  217.4 37.7 %copy-start.4 = (s32[128,8]{0,1:T(8,128)S(1)}, s32[128,8]{0,1:T(8,128)}, u32[]{:S(2)}) copy-start(s32[128,8]{0,1:T(8,128)} %param.10) | copy-start | bytes 12292
  245.3 9.6 %all-to-all-start.1 = ((bf16[32,1,80]{2,1,0:T(2,128)(2,1)}), bf16[32,1,80]{2,1,0:T(2,128)(2,1)S(1)}, u32[]{:S(2)}, u32[]{:S(2)}) async-start(bf16[32,1,80]{2,1,0:T(2,128)(2,1)} %convert_element_type.73), calls=%async_computation.1 | async-start | bytes 32768 | tf_op jit(solution)/shard_map/all_to_all | solution.py:380
  264.9 129.6 %copy-start.1 = (bf16[128,3584]{1,0:T(8,128)(2,1)S(1)}, bf16[128,3584]{1,0:T(8,128)(2,1)}, u32[]{:S(2)}) copy-start(bf16[128,3584]{1,0:T(8,128)(2,1)} %param.8) | copy-start | bytes 2752516

commit v2 on v1

--- a/solution.py
+++ b/solution.py
@@ -11,6 +11,7 @@
 MESH = pl.DeviceIdType.MESH
 GROUPS = 4
 PEERS = 8
+LANES = 128
 MIB = 1024 * 1024
 
 
@@ -61,107 +62,189 @@
         pl.semaphore_wait(sem, GROUPS + 2)
 
 
-def dispatch_kernel(tok, grad, ytok, ygrad, local_sem, zs, zr, ss, rs):
+def dispatch_kernel(
+    rows, tok, grad, up_hbm, down_hbm, ytok, ygrad, inner, gate_out,
+    up, down, tok_buf, grad_buf, raised, gate, total,
+    local_sem, weight_sem, load_sem, zs, zr, ss, rs,
+):
     at = Place()
+    g, d = at.group, at.dev
+    tile = 256
+    features, hidden = up.shape
+    up_load = pltpu.make_async_copy(up_hbm, up, weight_sem.at[0])
+    down_load = pltpu.make_async_copy(down_hbm, down, weight_sem.at[1])
     at.barrier()
     pairs = ((tok, ytok), (grad, ygrad))
-    g, d = at.group, at.dev
+
+    def lines_of(origin):
+        return pl.ds(pl.multiple_of(origin * rows, 16), rows)
 
     def local(a):
         src, dst = pairs[a]
-        return pltpu.make_async_copy(src.at[g], dst.at[g, d], local_sem.at[a])
+        return pltpu.make_async_copy(src.at[g], dst.at[g, lines_of(d)], local_sem.at[a])
 
     def zcopy(a, k):
         src, dst = pairs[a]
         target = lax.rem(g + GROUPS - k, GROUPS)
         return pltpu.make_async_remote_copy(
-            src_ref=src.at[target], dst_ref=dst.at[g, d],
+            src_ref=src.at[target], dst_ref=dst.at[g, lines_of(d)],
             send_sem=zs.at[a, k], recv_sem=zr.at[a, k],
             device_id=(target, d), device_id_type=MESH,
         )
 
     def copy(a, k, origin, slot, rel, peer):
-        buf = pairs[a][1].at[at.source(k), origin]
+        buf = pairs[a][1].at[at.source(k), lines_of(origin)]
         return pltpu.make_async_remote_copy(
             src_ref=buf, dst_ref=buf,
             send_sem=ss.at[a, k, slot], recv_sem=rs.at[a, k, rel],
             device_id=(g, peer), device_id_type=MESH,
         )
 
-    def sends(a, k):
-        first = [
-            copy(a, k, d, 0, 2, at.xn),
-            copy(a, k, d, 1, 4, at.yn),
-            copy(a, k, d, 2, 1, at.sib),
-        ]
-        from_x = [copy(a, k, at.xn, 3, 3, at.sib)]
-        from_y = [copy(a, k, at.yn, 4, 5, at.sib)]
+    def far(a, k):
         if k % 2 == 0:
-            from_x.insert(0, copy(a, k, at.xn, 5, 6, at.yn))
-        else:
-            from_y.insert(0, copy(a, k, at.yn, 5, 6, at.xn))
-        last = [copy(a, k, at.diag, 6, 7, at.sib)]
-        return first, from_x, from_y, last
+            return copy(a, k, at.xn, 5, 6, at.yn)
+        return copy(a, k, at.yn, 5, 6, at.xn)
 
     def own(a, k):
         if k == 0:
             local(a).wait()
         else:
             zcopy(a, k).wait_recv()
-        for c in sends(a, k)[0]:
-            c.start()
+        copy(a, k, d, 0, 2, at.xn).start()
+        copy(a, k, d, 1, 4, at.yn).start()
+        copy(a, k, d, 2, 1, at.sib).start()
 
     def forward(a, k):
-        parts = sends(a, k)
         copy(a, k, at.xn, 0, 2, at.xn).wait_recv()
-        for c in parts[1]:
-            c.start()
+        if k % 2 == 0:
+            far(a, k).start()
+        copy(a, k, at.xn, 3, 3, at.sib).start()
         copy(a, k, at.yn, 1, 4, at.yn).wait_recv()
-        for c in parts[2]:
-            c.start()
+        if k % 2 == 1:
+            far(a, k).start()
+        copy(a, k, at.yn, 4, 5, at.sib).start()
 
     def forward_last(a, k):
         copy(a, k, at.diag, 5, 6, at.xn).wait_recv()
-        for c in sends(a, k)[3]:
-            c.start()
+        copy(a, k, at.diag, 6, 7, at.sib).start()
+
+    def load(a, k):
+        buf = tok_buf if a == 0 else grad_buf
+        return pltpu.make_async_copy(pairs[a][1].at[at.source(k)], buf, load_sem.at[a])
+
+    def finish(a, k):
+        copy(a, k, at.sib, 2, 1, at.sib).wait_recv()
+        copy(a, k, at.xn + at.off_sib, 3, 3, at.sib).wait_recv()
+        copy(a, k, at.yn + at.off_sib, 4, 5, at.sib).wait_recv()
+        copy(a, k, at.diag + at.off_sib, 6, 7, at.sib).wait_recv()
+        load(a, k).start()
+
+    def raise_rows(k):
+        mine = lax.broadcasted_iota(jnp.int32, gate.shape[1:], 1) == d
+        held = jnp.where(mine, tok_buf[:, features:].astype(jnp.float32), 0.0)
+        gate[k] = jnp.broadcast_to(jnp.sum(held, axis=1, keepdims=True), gate.shape[1:])
+
+        @pl.loop(0, hidden // tile)
+        def _(n):
+            cols = pl.ds(pl.multiple_of(n * tile, tile), tile)
+            raised[k, :, cols] = jnp.dot(
+                tok_buf[:, :features], up[:, cols], preferred_element_type=jnp.float32
+            )
+
+    def lower_rows(k):
+        total[...] = jnp.zeros_like(total)
+
+        @pl.loop(0, hidden // tile)
+        def _(n):
+            cols = pl.ds(pl.multiple_of(n * tile, tile), tile)
+            backward = lax.dot_general(
+                grad_buf[...], down[cols, :], (((1,), (1,)), ((), ())),
+                preferred_element_type=jnp.float32,
+            )
+            value = raised[k, :, cols]
+            sig = jax.nn.sigmoid(value)
+            terms = value * sig * backward
+            total[...] += terms[:, :128] + terms[:, 128:]
+            slope = sig * (1.0 + value * (1.0 - sig))
+            inner[at.source(k), :, cols] = (gate[k][:, :1] * backward * slope).astype(
+                jnp.bfloat16
+            )
+
+        mine = lax.broadcasted_iota(jnp.int32, total.shape, 1) == d
+        summed = jnp.sum(total[...], axis=1, keepdims=True)
+        gate_out[at.source(k)] = jnp.where(mine, summed, 0.0).astype(jnp.bfloat16)
+
+    def compute(a, k):
+        load(a, k).wait()
+        if (a, k) == order[0]:
+            up_load.wait()
+        if (a, k) == order[1]:
+            down_load.wait()
+        if a == 0:
+            raise_rows(k)
+        else:
+            lower_rows(k)
 
     order = [(0, 0), (1, 0), (0, 1), (0, 2), (0, 3), (1, 1), (1, 2), (1, 3)]
+    steps = len(order)
     for a in range(2):
         local(a).start()
     for k in range(1, GROUPS):
         zcopy(0, k).start()
-    for i in range(len(order) + 2):
-        if i < len(order):
+    for i in range(steps + 4):
+        if i < steps:
             own(*order[i])
         if i == 1:
             for k in range(1, GROUPS):
                 zcopy(1, k).start()
-        if 1 <= i <= len(order):
+            up_load.start()
+            down_load.start()
+        if 1 <= i <= steps:
             forward(*order[i - 1])
-        if i >= 2:
+        if 2 <= i <= steps + 1:
             forward_last(*order[i - 2])
+        if i >= 4:
+            compute(*order[i - 4])
+        if 3 <= i <= steps + 2:
+            finish(*order[i - 3])
     for a, k in order:
-        copy(a, k, at.sib, 2, 1, at.sib).wait_recv()
-        copy(a, k, at.xn + at.off_sib, 3, 3, at.sib).wait_recv()
-        copy(a, k, at.yn + at.off_sib, 4, 5, at.sib).wait_recv()
-        copy(a, k, at.diag + at.off_sib, 6, 7, at.sib).wait_recv()
-        for part in sends(a, k):
-            for c in part:
-                c.wait_send()
+        copy(a, k, d, 0, 2, at.xn).wait_send()
+        copy(a, k, d, 1, 4, at.yn).wait_send()
+        copy(a, k, d, 2, 1, at.sib).wait_send()
+        copy(a, k, at.xn, 3, 3, at.sib).wait_send()
+        copy(a, k, at.yn, 4, 5, at.sib).wait_send()
+        far(a, k).wait_send()
+        copy(a, k, at.diag, 6, 7, at.sib).wait_send()
         if k:
             zcopy(a, k).wait_send()
 
 
-def dispatch(tok, grad):
-    groups, rows, features = tok.shape
-    out = jax.ShapeDtypeStruct((groups, PEERS, rows, features), jnp.bfloat16)
+def dispatch(tok, grad, up_matrix, down_matrix):
+    groups, rows, wide = tok.shape
+    features, hidden = up_matrix.shape
+    lines = PEERS * rows
     anywhere = pl.BlockSpec(memory_space=pl.ANY)
+    whole = pl.BlockSpec(memory_space=pltpu.VMEM)
     return pl.pallas_call(
-        dispatch_kernel,
-        out_shape=(out, out),
-        in_specs=[anywhere, anywhere],
-        out_specs=(anywhere, anywhere),
+        functools.partial(dispatch_kernel, rows),
+        out_shape=(
+            jax.ShapeDtypeStruct((groups, lines, wide), jnp.bfloat16),
+            jax.ShapeDtypeStruct((groups, lines, features), jnp.bfloat16),
+            jax.ShapeDtypeStruct((groups, lines, hidden), jnp.bfloat16),
+            jax.ShapeDtypeStruct((groups, lines, LANES), jnp.bfloat16),
+        ),
+        in_specs=[anywhere] * 4,
+        out_specs=(anywhere, anywhere, whole, whole),
         scratch_shapes=[
+            pltpu.VMEM((features, hidden), jnp.bfloat16),
+            pltpu.VMEM((hidden, features), jnp.bfloat16),
+            pltpu.VMEM((lines, wide), jnp.bfloat16),
+            pltpu.VMEM((lines, features), jnp.bfloat16),
+            pltpu.VMEM((groups, lines, hidden), jnp.float32),
+            pltpu.VMEM((groups, lines, LANES), jnp.float32),
+            pltpu.VMEM((lines, LANES), jnp.float32),
+            pltpu.SemaphoreType.DMA((2,)),
+            pltpu.SemaphoreType.DMA((2,)),
             pltpu.SemaphoreType.DMA((2,)),
             pltpu.SemaphoreType.DMA((2, GROUPS)),
             pltpu.SemaphoreType.DMA((2, GROUPS)),
@@ -169,13 +252,13 @@
             pltpu.SemaphoreType.DMA((2, GROUPS, 8)),
         ],
         compiler_params=pltpu.CompilerParams(
-            collective_id=0, has_side_effects=True, vmem_limit_bytes=4 * MIB
-        ),
-    )(tok, grad)
+            collective_id=0, has_side_effects=True, vmem_limit_bytes=58 * MIB
+        ),
+    )(tok, grad, up_matrix, down_matrix)
 
 
 def combine_kernel(
-    rows, inner, up, out, part, sib, dbuf, xbuf, ybuf, local_sem, zs, zr, ss, rs, ps, pr
+    rows, inner, gates, up, out, part, sib, dbuf, xbuf, ybuf, local_sem, zs, zr, ss, rs, ps, pr
 ):
     at = Place()
     g, d = at.group, at.dev
@@ -194,6 +277,8 @@
                 preferred_element_type=jnp.float32,
             ).astype(jnp.bfloat16)
             part[k, :, :, cols] = block.reshape(PEERS, rows, tile)
+
+        part[k, :, :, features:] = gates[at.source(k)].reshape(PEERS, rows, LANES)
 
     chips = (at.dev, at.xn, at.yn, at.diag)
 
@@ -300,18 +385,18 @@
     local().wait()
 
 
-def combine(inner, up_matrix, rows):
-    features = up_matrix.shape[0]
+def combine(inner, gates, up_matrix, rows):
+    wide = up_matrix.shape[0] + LANES
     whole = pl.BlockSpec(memory_space=pltpu.VMEM)
-    hop = pltpu.VMEM((GROUPS, rows, features), jnp.bfloat16)
+    hop = pltpu.VMEM((GROUPS, rows, wide), jnp.bfloat16)
     return pl.pallas_call(
         functools.partial(combine_kernel, rows),
-        out_shape=jax.ShapeDtypeStruct((GROUPS, rows, features), jnp.bfloat16),
-        in_specs=[whole, whole],
+        out_shape=jax.ShapeDtypeStruct((GROUPS, rows, wide), jnp.bfloat16),
+        in_specs=[whole, whole, whole],
         out_specs=pl.BlockSpec(memory_space=pl.ANY),
         scratch_shapes=[
-            pltpu.VMEM((GROUPS, PEERS, rows, features), jnp.bfloat16),
-            pltpu.VMEM((GROUPS, 4, rows, features), jnp.bfloat16),
+            pltpu.VMEM((GROUPS, PEERS, rows, wide), jnp.bfloat16),
+            pltpu.VMEM((GROUPS, 4, rows, wide), jnp.bfloat16),
             hop,
             hop,
             hop,
@@ -326,12 +411,11 @@
         compiler_params=pltpu.CompilerParams(
             collective_id=1, has_side_effects=True, vmem_limit_bytes=58 * MIB
         ),
-    )(inner, up_matrix)
+    )(inner, gates, up_matrix)
 
 
 def grouped(tokens, out_grad, gate_weights, expert_ids, slot_ids, up_weight, down_weight):
     rows_dev, features = tokens.shape
-    hidden = up_weight.shape[2]
     experts = GROUPS * PEERS
     rows = 5 * rows_dev // 8
     up_matrix = up_weight[0]
@@ -358,38 +442,28 @@
     gate_table = jnp.sum(
         jnp.where(names, gate_weights.astype(jnp.float32)[:, :, None], 0.0), axis=1
     ).astype(jnp.bfloat16)
+    gate_lanes = jnp.pad(
+        gate_table.reshape(rows_dev, GROUPS, PEERS), ((0, 0), (0, 0), (0, LANES - PEERS))
+    )
     gate_send = jnp.einsum(
-        "tgp,tge->gep", pick, gate_table.reshape(rows_dev, GROUPS, PEERS),
-        preferred_element_type=jnp.float32,
+        "tgp,tge->gpe", pick, gate_lanes, preferred_element_type=jnp.float32
     ).astype(jnp.bfloat16)
-    gate_rows = lax.all_to_all(
-        gate_send.reshape(experts, rows), ("group", "dev"), 0, 0, tiled=True
-    ).reshape(-1)
-    token_rows, grad_rows = dispatch(packed(tokens), packed(out_grad))
-    raised = jnp.dot(
-        token_rows.reshape(-1, features), up_matrix, preferred_element_type=jnp.float32
-    )
-    backward = lax.dot_general(
-        grad_rows.reshape(-1, features), down_matrix, (((1,), (1,)), ((), ())),
-        preferred_element_type=jnp.float32,
-    )
-    gate_out = jnp.sum(jax.nn.silu(raised) * backward, axis=1).astype(jnp.bfloat16)
-    inner = (gate_rows.astype(jnp.float32)[:, None] * backward * silu_slope(raised)).astype(
-        jnp.bfloat16
-    )
-    gate_back = lax.all_to_all(
-        gate_out.reshape(experts, rows), ("group", "dev"), 0, 0, tiled=True
-    )
-    halves = combine(inner.reshape(GROUPS, PEERS * rows, hidden), up_matrix, rows)
+    inner, gates = dispatch(
+        jnp.concatenate([packed(tokens), gate_send], axis=2),
+        packed(out_grad),
+        up_matrix,
+        down_matrix,
+    )[2:]
+    halves = combine(inner, gates, up_matrix, rows)
     gate_tokens = jnp.einsum(
-        "tgp,gep->tge", pick, gate_back.reshape(GROUPS, PEERS, rows),
+        "tgp,gpe->tge", pick, halves[:, :, features : features + PEERS],
         preferred_element_type=jnp.float32,
     ).reshape(rows_dev, experts)
     gate_grad = jnp.sum(jnp.where(names, gate_tokens[:, None, :], 0.0), axis=2).astype(
         jnp.bfloat16
     )
     token_grad = jnp.einsum(
-        "tgp,gpd->td", pick, halves, preferred_element_type=jnp.float32
+        "tgp,gpd->td", pick, halves[:, :, :features], preferred_element_type=jnp.float32
     ).astype(jnp.bfloat16)
     return (token_grad, gate_grad)
 

time: 395 us -> 345 us (0.87)
  matrix products: 65.8 us -> 7.61 us
  Pallas kernels: 289 us -> 332 us
  blocking collectives: 8.85 us -> 0 us
  other arithmetic: 13 us -> 4.46 us
  local copies, waits for them, and re-layouts: 7.32 us -> 0.21 us
  waiting for transfers between devices: 7.05 us -> 0 us
    dot_general x5 -> x3, matrix products: 63.1 us -> 4.52 us  [the longest x1 3.27 us: grouped(): jnp.einsum('tgp,gpd->td', pick, halves[:, :, :features], preferred_elemen...]
    pallas_call x1, Pallas kernels: 174 us -> 216 us  [dispatch(): pl.pallas_call(functools.partial(dispatch_kernel, rows), out_shape=(jax.S...]
    convert_element_type x2 -> x0, other arithmetic: 11.6 us -> none  [the longest x1 11.5 us: grouped(): (gate_rows.astype(jnp.float32)[:, None] * backward * silu_slope(raised))....]
    all_to_all x1 -> x0, blocking collectives: 8.85 us -> none  [grouped(): lax.all_to_all(gate_send.reshape(experts, rows), ('group', 'dev'), 0, 0,...]
    all_to_all x1 -> x0, waiting for transfers between devices: 7.05 us -> none  [grouped(): lax.all_to_all(gate_out.reshape(experts, rows), ('group', 'dev'), 0, 0, t...]
    unnamed x12 -> x8, local copies, waits for them, and re-layouts: 6.53 us -> 0.03 us
  transfers between devices with their start and end apart: 1 -> 0, of which waited for: 1 -> 0; matrix products, arithmetic and copies ran while one was open for 0% -> 0% of each run, Pallas kernels for 0% -> 0%
where the time goes in v2:
time: 345 us
  Pallas kernels  332 us (96%)
  matrix products  7.61 us (2%)
  other arithmetic  4.46 us (1%)
    pallas_call x1, Pallas kernels, dispatch(): pl.pallas_call(functools.partial(dispatch_kernel, rows), out_shape=(jax.S...  216 us
    pallas_call x1, Pallas kernels, combine(): pl.pallas_call(functools.partial(combine_kernel, rows), out_shape=jax.Sha...  116 us

profile of v2, /device:TPU:0, one launch (start us, length us, event | category | flops | bytes accessed | tf_op | source)
XLA Modules:
  0.0 344.9 jit_solution(10474107905368537171)
XLA Ops:
  0.6 0.0 copy-start
  0.6 0.0 copy-start.2
  0.7 0.8 convert_element_type.35
  1.5 0.7 select_reduce_fusion.1
  2.2 0.7 add_select_fusion
  2.9 0.1 convolution_convert_fusion.3
  3.0 0.2 copy.19
  3.2 0.2 convolution_convert_fusion.2
  3.4 0.0 copy-done
  3.4 2.2 convolution_convert_fusion.grad
  5.6 0.0 copy-done.2
  5.6 0.7 convolution_convert_fusion.1
  6.4 1.6 pad_maximum_fusion.tok
  8.0 215.5 %shard_map.77 = (bf16[4,640,3712]{2,1,0:T(8,128)(2,1)}, bf16[4,640,3584]{2,1,0:T(8,128)(2,1)}, bf16[4,640,1024]{2,1,0:T(8,128)(2,1)}, bf16[4,640,128]{2,1,0:T(8,128)(2,1)}) custom-call(bf16[4,80,3712]{2,1,0:T(8,128)(2,1)} %pad_maximum_fusion.tok, bf16[4,80,3584]{2,1,0:T(8,128)(2,1)} %convolution_convert_fusion.grad, bf16[3584,1024]{1,0:T(8,128)(2,1)} %bitcast.20, ...), custom_call_target="tpu_custom_call" | custom-call | tf_op jit(solution)/shard_map/pallas_call | solution.py:228
  223.5 0.0 copy-start.1
  223.5 116.3 %shard_map.78 = bf16[4,80,3712]{2,1,0:T(8,128)(2,1)} custom-call(bf16[4,640,1024]{2,1,0:T(8,128)(2,1)} %get-tuple-element.4.inner, bf16[4,640,128]{2,1,0:T(8,128)(2,1)} %get-tuple-element.5.gates, bf16[3584,1024]{1,0:T(8,128)(2,1)} %bitcast.21), custom_call_target="tpu_custom_call" | custom-call | tf_op jit(solution)/shard_map/pallas_call | solution.py:392
  339.9 0.0 copy-start.3
  339.9 1.1 convolution_bitcast_fusion.1
  341.0 3.3 fusion
  344.3 0.0 copy-done.3
  344.3 0.6 select_reduce_fusion
  344.9 0.0 copy-done.1
  (1 shorter events, 0.0 us)
Async XLA Ops:
  0.6 2.8 copy-start
  0.6 5.0 %copy-start.2 = (bf16[128,3584]{1,0:T(8,128)(2,1)S(1)}, bf16[128,3584]{1,0:T(8,128)(2,1)}, u32[]{:S(2)}) copy-start(bf16[128,3584]{1,0:T(8,128)(2,1)} %param.7) | copy-start | bytes 2752516
  223.5 121.3 %copy-start.1 = (bf16[128,3584]{1,0:T(8,128)(2,1)S(1)}, bf16[128,3584]{1,0:T(8,128)(2,1)}, u32[]{:S(2)}) copy-start(bf16[128,3584]{1,0:T(8,128)(2,1)} %param.8) | copy-start | bytes 2752516
  339.9 4.4 %copy-start.3 = (s32[128,8]{0,1:T(8,128)S(1)}, s32[128,8]{0,1:T(8,128)}, u32[]{:S(2)}) copy-start(s32[128,8]{0,1:T(8,128)} %param.10) | copy-start | bytes 12292

commit v3 on v2

--- a/solution.py
+++ b/solution.py
@@ -191,7 +191,7 @@
         local(a).start()
     for k in range(1, GROUPS):
         zcopy(0, k).start()
-    for i in range(steps + 4):
+    for i in range(steps + 2):
         if i < steps:
             own(*order[i])
         if i == 1:
@@ -201,12 +201,10 @@
             down_load.start()
         if 1 <= i <= steps:
             forward(*order[i - 1])
-        if 2 <= i <= steps + 1:
+        if i >= 2:
             forward_last(*order[i - 2])
-        if i >= 4:
-            compute(*order[i - 4])
-        if 3 <= i <= steps + 2:
-            finish(*order[i - 3])
+            finish(*order[i - 2])
+            compute(*order[i - 2])
     for a, k in order:
         copy(a, k, d, 0, 2, at.xn).wait_send()
         copy(a, k, d, 1, 4, at.yn).wait_send()
@@ -363,16 +361,15 @@
             local().start()
 
     order = (2, 1, 3, 0)
-    for i in range(len(order) + 3):
+    for i in range(len(order) + 2):
         if i < len(order):
             product(order[i])
             start_pairs(order[i])
+            first(order[i])
         if 1 <= i <= len(order):
-            first(order[i - 1])
-        if 2 <= i <= len(order) + 1:
-            second(order[i - 2])
-        if i >= 3:
-            third(order[i - 3])
+            second(order[i - 1])
+        if i >= 2:
+            third(order[i - 2])
     for k in order:
         for i in range(4):
             pair(k, i).wait_send()

time: 345 us -> 352 us (1.020)
  Pallas kernels: 332 us -> 338 us
    pallas_call x1, Pallas kernels: 116 us -> 127 us  [combine(): pl.pallas_call(functools.partial(combine_kernel, rows), out_shape=jax.Sha...]
    pallas_call x1, Pallas kernels: 216 us -> 211 us  [dispatch(): pl.pallas_call(functools.partial(dispatch_kernel, rows), out_shape=(jax.S...]
where the time goes in v3:
time: 352 us; the launch traced here: 351 us
  Pallas kernels  338 us (96%)
  matrix products  7.61 us (2%)
  other arithmetic  4.46 us (1%)
    pallas_call x1, Pallas kernels, dispatch(): pl.pallas_call(functools.partial(dispatch_kernel, rows), out_shape=(jax.S...  211 us
    pallas_call x1, Pallas kernels, combine(): pl.pallas_call(functools.partial(combine_kernel, rows), out_shape=jax.Sha...  127 us

profile of v3, /device:TPU:0, one launch (start us, length us, event | category | flops | bytes accessed | tf_op | source)
XLA Modules:
  0.0 351.0 jit_solution(10989508885087573727)
XLA Ops:
  0.6 0.0 copy-start
  0.6 0.0 copy-start.2
  0.7 0.8 convert_element_type.35
  1.5 0.7 select_reduce_fusion.1
  2.2 0.7 add_select_fusion
  2.9 0.1 convolution_convert_fusion.3
  3.0 0.2 copy.19
  3.2 0.2 convolution_convert_fusion.2
  3.4 0.0 copy-done
  3.4 2.2 convolution_convert_fusion.grad
  5.6 0.0 copy-done.2
  5.6 0.7 convolution_convert_fusion.1
  6.4 1.6 pad_maximum_fusion.tok
  8.0 210.7 %shard_map.77 = (bf16[4,640,3712]{2,1,0:T(8,128)(2,1)}, bf16[4,640,3584]{2,1,0:T(8,128)(2,1)}, bf16[4,640,1024]{2,1,0:T(8,128)(2,1)}, bf16[4,640,128]{2,1,0:T(8,128)(2,1)}) custom-call(bf16[4,80,3712]{2,1,0:T(8,128)(2,1)} %pad_maximum_fusion.tok, bf16[4,80,3584]{2,1,0:T(8,128)(2,1)} %convolution_convert_fusion.grad, bf16[3584,1024]{1,0:T(8,128)(2,1)} %bitcast.20, ...), custom_call_target="tpu_custom_call" | custom-call | tf_op jit(solution)/shard_map/pallas_call | solution.py:226
  218.7 0.0 copy-start.1
  218.7 127.4 %shard_map.78 = bf16[4,80,3712]{2,1,0:T(8,128)(2,1)} custom-call(bf16[4,640,1024]{2,1,0:T(8,128)(2,1)} %get-tuple-element.4.inner, bf16[4,640,128]{2,1,0:T(8,128)(2,1)} %get-tuple-element.5.gates, bf16[3584,1024]{1,0:T(8,128)(2,1)} %bitcast.21), custom_call_target="tpu_custom_call" | custom-call | tf_op jit(solution)/shard_map/pallas_call | solution.py:389
  346.1 0.0 copy-start.3
  346.1 1.1 convolution_bitcast_fusion.1
  347.2 3.3 fusion
  350.4 0.0 copy-done.3
  350.4 0.6 select_reduce_fusion
  351.0 0.0 copy-done.1
  (1 shorter events, 0.0 us)
Async XLA Ops:
  0.6 2.8 copy-start
  0.6 5.0 %copy-start.2 = (bf16[128,3584]{1,0:T(8,128)(2,1)S(1)}, bf16[128,3584]{1,0:T(8,128)(2,1)}, u32[]{:S(2)}) copy-start(bf16[128,3584]{1,0:T(8,128)(2,1)} %param.7) | copy-start | bytes 2752516
  218.7 132.4 %copy-start.1 = (bf16[128,3584]{1,0:T(8,128)(2,1)S(1)}, bf16[128,3584]{1,0:T(8,128)(2,1)}, u32[]{:S(2)}) copy-start(bf16[128,3584]{1,0:T(8,128)(2,1)} %param.8) | copy-start | bytes 2752516
  346.1 4.4 %copy-start.3 = (s32[128,8]{0,1:T(8,128)S(1)}, s32[128,8]{0,1:T(8,128)}, u32[]{:S(2)}) copy-start(s32[128,8]{0,1:T(8,128)} %param.10) | copy-start | bytes 12292
